TPU v7x, 32 devices: a whole 2x2x4 slice. The times are simulated.
32 devices in a mesh: pool: 2 (over x), row: 8 (over z, y), col: 2 (over core).
Axes of the slice: x: 2, y: 2, z: 4, core: 2. Of those that a mesh axis runs over, the one named last changes fastest.
Arguments:
- grad_slots: bfloat16 [48, 256, 14336], P(('pool', 'row'), 'col'), parts along dimension 0, may hold values from -6 to 6
- block_owner: int32 [32], P('pool'), parts along dimension 0, may hold values from 0 to 7, as said below
- factor: bfloat16 [8192, 4096], P(('pool', 'col'), 'row'), parts along dimension 0, may hold values from -0.125 to 0.125
- pattern: int32 [16, 8], P('pool'), parts along dimension 0, may hold values from 0 to 1, as said below
Outputs:
- precond: bfloat16 [8192, 14336], P(('pool', 'col'), 'row'), parts along dimension 0
There are 2 independent parts, one for each index of `pool`. A program takes and returns all parts, laid end to end along the dimension named above; each array names one. Nothing has to cross between parts.
Inputs may be any that keep to these rules, and one draw needn't show every extreme that they name: `block_owner`: no trainer shard holds more than 3 blocks and one holds exactly 3; a shard keeps its blocks in its first slots in increasing block order, and the other slots are unused. `pattern`: 1 on the diagonal and 0 below it.
All inputs are finite; a program needn't handle non-finite values.
Results may differ from a plain program's by a relative error of at most 0.004.
Values may be sent and summed in bfloat16 or wider, within the bound.
A program may use at most 192 MiB of HBM per device.

v0:
```python
import jax
import jax.numpy as jnp
from jax import lax
from jax.sharding import PartitionSpec as P


def body(grad_slots, block_owner, factor, pattern):
    row_idx = lax.axis_index("row")
    col_idx = lax.axis_index("col")
    slot_cap = grad_slots.shape[0]
    block_total = block_owner.shape[0]
    received = lax.all_to_all(grad_slots, "row", split_axis=2, concat_axis=0, tiled=True)
    same_owner = block_owner[:, None] == block_owner[None, :]
    earlier = jnp.arange(block_total)[None, :] < jnp.arange(block_total)[:, None]
    owner_rank = jnp.sum(same_owner & earlier, axis=1)
    slot_of = block_owner * slot_cap + owner_rank
    picked = jnp.take(received, slot_of, axis=0)
    blocks = lax.all_gather(picked, "col", axis=1, tiled=True)
    grad_cols = blocks.reshape(-1, blocks.shape[2])
    half_rows, piece_width = factor.shape
    block_count = pattern.shape[0]
    total_rows = 2 * half_rows
    block_size = total_rows // block_count
    half_blocks = block_count // 2
    col_block = (row_idx * piece_width + jnp.arange(piece_width)) // block_size
    row_blocks = col_idx * half_blocks + jnp.arange(half_blocks)
    sel_cols = (jnp.arange(block_count)[:, None] == col_block[None, :]).astype(jnp.float32)
    pattern_cols = jnp.dot(pattern.astype(jnp.float32), sel_cols)
    sel_rows = (row_blocks[:, None] == jnp.arange(block_count)[None, :]).astype(jnp.float32)
    block_mask = jnp.dot(sel_rows, pattern_cols)
    keep_mask = block_mask > 0.5
    shaped = factor.reshape(half_blocks, block_size, piece_width)
    masked = jnp.where(keep_mask[:, None, :], shaped, jnp.zeros_like(shaped)).reshape(
        half_rows, piece_width
    )
    result = jnp.dot(
        lax.all_gather(masked, "row", axis=1, tiled=True),
        grad_cols,
        preferred_element_type=jnp.float32,
    )
    return result.astype(jnp.bfloat16)


def solution(mesh):
    placed = (
        P(("pool", "row"), "col", None),
        P("pool"),
        P(("pool", "col"), "row"),
        P("pool", None),
    )
    return jax.shard_map(
        body, mesh=mesh, in_specs=placed, out_specs=P(("pool", "col"), "row"), check_vma=False
    )
```

profile of v0, /device:TPU:0, one launch (start us, length us, event | category | flops | bytes accessed | tf_op | source)
XLA Modules:
  0.0 657.5 jit_solution(4763586861439865328)
XLA Ops:
  6.5 0.0 all-gather.3.cloned.1.call-start
  6.6 0.9 fusion.3
  7.5 3.1 bitcast_select_fusion
  10.6 0.0 all-gather.3.cloned.1.call-update
  10.6 22.4 %copy.10 = bf16[3,128,14336]{1,0,2:T(4,128)(2,1)} copy(bf16[3,128,14336]{2,1,0:T(8,128)(2,1)} %param.4) | data formatting | bytes 22020096 | tf_op args[0]
  33.0 0.0 copy-start
  33.0 7.4 %all-to-all-start = ((bf16[3,128,14336]{1,0,2:T(4,128)(2,1)}), bf16[3,128,14336]{1,0,2:T(4,128)(2,1)}, u32[]{:S(2)}, u32[]{:S(2)}) async-start(bf16[3,128,14336]{1,0,2:T(4,128)(2,1)} %copy.10), calls=%async_computation | async-start | bytes 29360128 | tf_op jit(solution)/shard_map/all_to_all | solution.py:12
  40.4 0.0 all-gather.5.cloned.1.call-start
  40.5 0.0 copy-done
  40.5 0.2 convert_reduce_fusion
  40.7 504.1 %all-to-all-done = bf16[3,128,14336]{1,0,2:T(4,128)(2,1)} async-done(((bf16[3,128,14336]{1,0,2:T(4,128)(2,1)}), bf16[3,128,14336]{1,0,2:T(4,128)(2,1)}, u32[]{:S(2)}, u32[]{:S(2)}) %all-to-all-start) | async-done | bytes 11010080 | tf_op jit(solution)/shard_map/all_to_all | solution.py:12
  544.8 12.4 %copy.11 = bf16[3,128,14336]{1,2,0:T(8,128)(2,1)} copy(bf16[3,128,14336]{1,0,2:T(4,128)(2,1)} %all-to-all-done) | data formatting | bytes 22020096 | tf_op jit(solution)/shard_map/all_to_all | solution.py:12
  557.2 14.2 %copy.12 = bf16[8,3,128,1792]{3,2,1,0:T(8,128)(2,1)} copy(bf16[8,3,128,1792]{2,3,0,1:T(8,128)(2,1)} %bitcast.9) | data formatting | bytes 22020096 | tf_op jit(solution)/shard_map/all_to_all | solution.py:12
  571.3 8.2 %gather_fusion = bf16[16,128,1792]{2,1,0:T(8,128)(2,1)} fusion(bf16[24,128,1792]{2,1,0:T(8,128)(2,1)} %bitcast.10, s32[1024]{0:T(1024)S(1)} %pad_clamp_fusion), kind=kCustom, calls=%fused_computation | custom fusion | bytes 14680128 | tf_op jit(solution)/shard_map/jit(_take)/gather | solution.py:17
  579.5 6.9 %broadcast_select_fusion = bf16[16,128,1792]{2,1,0:T(8,128)(2,1)} fusion(bf16[16,128,1792]{2,1,0:T(8,128)(2,1)} %gather_fusion, pred[16]{0:T(512)(128)(4,1)S(1)} %get-tuple-element.5), kind=kLoop, calls=%fused_computation.2 | loop fusion | flops 3670016 | bytes 14680080 | tf_op jit(solution)/shard_map/jit(_take)/select_n | solution.py:17
  586.4 0.0 all-gather.5.cloned.1.call-update
  586.5 0.0 all-gather.3.cloned.1.call-done
  586.5 25.5 %all-gather.5.cloned.1.call-done = bf16[16,256,1792]{2,1,0:T(8,128)(2,1)} async-done(((bf16[16,128,1792]{2,1,0:T(8,128)(2,1)}), bf16[16,256,1792]{2,1,0:T(8,128)(2,1)}) %all-gather.5.cloned.1.call-update) | async-done | bytes 14680080 | tf_op jit(solution)/shard_map/all_gather | solution.py:18
  612.0 38.6 %convolution_convert_fusion = bf16[2048,1792]{1,0:T(8,128)(2,1)} fusion(bf16[2048,4096]{1,0:T(8,128)(2,1)} %all-gather.3.cloned.1.call-done, bf16[4096,1792]{1,0:T(8,128)(2,1)} %bitcast.11), kind=kOutput, calls=%fused_computation.1 | convolution fusion | flops 30068441088 | bytes 38797312 | tf_op jit(solution)/shard_map/dot_general | solution.py:36
  (4 shorter events, 0.0 us)
Async XLA Ops:
  6.5 579.9 %all-gather.3.cloned.1.call-start = ((), (), s32[]{:S(2)}) async-start(), calls=%async_computation.1 | async-start | bytes 18874368 | tf_op jit(solution)/shard_map/all_gather | solution.py:37
  33.0 7.5 %copy-start = (s32[16]{0:T(128)S(1)}, s32[16]{0:T(128)}, u32[]{:S(2)}) copy-start(s32[16]{0:T(128)} %param.5) | copy-start | bytes 196
  33.0 511.8 %all-to-all-start = ((bf16[3,128,14336]{1,0,2:T(4,128)(2,1)}), bf16[3,128,14336]{1,0,2:T(4,128)(2,1)}, u32[]{:S(2)}, u32[]{:S(2)}) async-start(bf16[3,128,14336]{1,0,2:T(4,128)(2,1)} %copy.10), calls=%async_computation | async-start | bytes 29360128 | tf_op jit(solution)/shard_map/all_to_all | solution.py:12
  40.4 571.6 %all-gather.5.cloned.1.call-start = ((), (), s32[]{:S(2)}) async-start(), calls=%async_computation.2 | async-start | bytes 22020096 | tf_op jit(solution)/shard_map/all_gather | solution.py:18
Sparse Core Ops, SparseCore 0:
  10.7 526.6 all-gather.2
  586.6 25.3 all-gather.4
where the time goes:
time: 659 us; the launch traced here: 657 us
  waiting for transfers between devices  530 us (80%)
  local copies, waits for them, and re-layouts  57.2 us (9%)
  matrix products  39.5 us (6%)
  between operations  13.4 us (2%)
  other arithmetic  10.2 us (2%)
  starting transfers between devices  7.44 us (1%)
    all_to_all x1, waiting for transfers between devices, body(): lax.all_to_all(grad_slots, 'row', split_axis=2, concat_axis=0, tiled=True)  504 us
    dot_general x1, matrix products, body(): jnp.dot(lax.all_gather(masked, 'row', axis=1, tiled=True), grad_cols, pre...  38.6 us
    all_to_all x2, local copies, waits for them, and re-layouts, body(): lax.all_to_all(grad_slots, 'row', split_axis=2, concat_axis=0, tiled=True)  26.6 us
    all_gather x1, waiting for transfers between devices, body(): blocks = lax.all_gather(picked, 'col', axis=1, tiled=True)  25.5 us
    unnamed x3, local copies, waits for them, and re-layouts  22.4 us
  transfers between devices with their start and end apart: 3, of which 2 were waited for; matrix products, arithmetic and copies ran while one was open for 10% of the time, Pallas kernels for 0%

commit v1 on v0

--- a/solution.py
+++ b/solution.py
@@ -9,7 +9,10 @@
     col_idx = lax.axis_index("col")
     slot_cap = grad_slots.shape[0]
     block_total = block_owner.shape[0]
-    received = lax.all_to_all(grad_slots, "row", split_axis=2, concat_axis=0, tiled=True)
+    received = jnp.concatenate(
+        lax.all_to_all(jnp.stack(jnp.split(grad_slots, lax.axis_size("row"), axis=2)), "row", 0, 0),
+        axis=0,
+    )
     same_owner = block_owner[:, None] == block_owner[None, :]
     earlier = jnp.arange(block_total)[None, :] < jnp.arange(block_total)[:, None]
     owner_rank = jnp.sum(same_owner & earlier, axis=1)

time: 659 us -> 545 us (0.83)
  waiting for transfers between devices: 530 us -> 444 us
  local copies, waits for them, and re-layouts: 57.2 us -> 28.8 us
    all_to_all x1, waiting for transfers between devices: 504 us -> 418 us  [body(): lax.all_to_all(jnp.stack(jnp.split(grad_slots, lax.axis_size('row'), axis...]
    all_to_all x2 -> x0, local copies, waits for them, and re-layouts: 26.6 us -> none  [body(): lax.all_to_all(grad_slots, 'row', split_axis=2, concat_axis=0, tiled=True)]
    unnamed x3 -> x9, local copies, waits for them, and re-layouts: 22.4 us -> 18.1 us
  transfers between devices with their start and end apart: 3 -> 3, of which waited for: 2 -> 2; matrix products, arithmetic and copies ran while one was open for 10% -> 7% of each run, Pallas kernels for 0% -> 0%
where the time goes in v1:
time: 545 us; the launch traced here: 544 us
  waiting for transfers between devices  444 us (81%)
  matrix products  39.7 us (7%)
  local copies, waits for them, and re-layouts  28.8 us (5%)
  between operations  13.4 us (2%)
  other arithmetic  10.2 us (2%)
  starting transfers between devices  7.58 us (1%)
    all_to_all x1, waiting for transfers between devices, body(): lax.all_to_all(jnp.stack(jnp.split(grad_slots, lax.axis_size('row'), axis...  418 us
    dot_general x1, matrix products, body(): jnp.dot(lax.all_gather(masked, 'row', axis=1, tiled=True), grad_cols, pre...  38.6 us
    all_gather x1, waiting for transfers between devices, body(): blocks = lax.all_gather(picked, 'col', axis=1, tiled=True)  26.6 us
    unnamed x9, local copies, waits for them, and re-layouts  18.1 us
  transfers between devices with their start and end apart: 3, of which 2 were waited for; matrix products, arithmetic and copies ran while one was open for 7% of the time, Pallas kernels for 0%

profile of v1, /device:TPU:0, one launch (start us, length us, event | category | flops | bytes accessed | tf_op | source)
XLA Modules:
  0.0 544.0 jit_solution(7315585157311805758)
XLA Ops:
  6.5 0.0 all-gather.3.cloned.1.call-start
  6.6 1.1 fusion.3
  7.7 3.1 bitcast_select_fusion
  10.7 0.0 all-gather.3.cloned.1.call-update
  10.7 2.5 bitcast_dynamic-update-slice_fusion.7
  13.3 2.6 bitcast_dynamic-update-slice_fusion.6
  15.8 2.5 bitcast_dynamic-update-slice_fusion.5
  18.4 2.5 bitcast_dynamic-update-slice_fusion.4
  20.9 2.8 bitcast_dynamic-update-slice_fusion.3
  23.6 2.6 bitcast_dynamic-update-slice_fusion.2
  26.2 2.6 bitcast_dynamic-update-slice_fusion.1
  28.8 2.5 bitcast_dynamic-update-slice_fusion
  31.3 0.0 copy-start
  31.3 7.5 %all-to-all-start = ((bf16[8,3,128,1792]{3,2,1,0:T(8,128)(2,1)}), bf16[8,3,128,1792]{3,2,1,0:T(8,128)(2,1)}, u32[]{:S(2)}, u32[]{:S(2)}) async-start(bf16[8,3,128,1792]{3,2,1,0:T(8,128)(2,1)} %bitcast_dynamic-update-slice_fusion), calls=%async_computation | async-start | bytes 22020096 | tf_op jit(solution)/shard_map/all_to_all | solution.py:13
  38.9 0.0 all-gather.5.cloned.1.call-start
  38.9 0.0 copy-done
  38.9 0.2 convert_reduce_fusion
  39.1 417.6 %all-to-all-done = bf16[8,3,128,1792]{3,2,1,0:T(8,128)(2,1)} async-done(((bf16[8,3,128,1792]{3,2,1,0:T(8,128)(2,1)}), bf16[8,3,128,1792]{3,2,1,0:T(8,128)(2,1)}, u32[]{:S(2)}, u32[]{:S(2)}) %all-to-all-start) | async-done | bytes 11010080 | tf_op jit(solution)/shard_map/all_to_all | solution.py:13
  456.8 8.2 %gather_fusion = bf16[16,128,1792]{2,1,0:T(8,128)(2,1)} fusion(bf16[24,128,1792]{2,1,0:T(8,128)(2,1)} %bitcast.9, s32[1024]{0:T(1024)S(1)} %pad_clamp_fusion), kind=kCustom, calls=%fused_computation | custom fusion | bytes 14680128 | tf_op jit(solution)/shard_map/jit(_take)/gather | solution.py:20
  465.0 6.9 %broadcast_select_fusion = bf16[16,128,1792]{2,1,0:T(8,128)(2,1)} fusion(bf16[16,128,1792]{2,1,0:T(8,128)(2,1)} %gather_fusion, pred[16]{0:T(512)(128)(4,1)S(1)} %get-tuple-element.5), kind=kLoop, calls=%fused_computation.2 | loop fusion | flops 3670016 | bytes 14680080 | tf_op jit(solution)/shard_map/jit(_take)/select_n | solution.py:20
  471.9 0.0 all-gather.5.cloned.1.call-update
  471.9 0.0 all-gather.3.cloned.1.call-done
  471.9 26.6 %all-gather.5.cloned.1.call-done = bf16[16,256,1792]{2,1,0:T(8,128)(2,1)} async-done(((bf16[16,128,1792]{2,1,0:T(8,128)(2,1)}), bf16[16,256,1792]{2,1,0:T(8,128)(2,1)}) %all-gather.5.cloned.1.call-update) | async-done | bytes 14680080 | tf_op jit(solution)/shard_map/all_gather | solution.py:21
  498.6 38.6 %convolution_convert_fusion = bf16[2048,1792]{1,0:T(8,128)(2,1)} fusion(bf16[2048,4096]{1,0:T(8,128)(2,1)} %all-gather.3.cloned.1.call-done, bf16[4096,1792]{1,0:T(8,128)(2,1)} %bitcast.22), kind=kOutput, calls=%fused_computation.1 | convolution fusion | flops 30068441088 | bytes 38797312 | tf_op jit(solution)/shard_map/dot_general | solution.py:39
  (4 shorter events, 0.0 us)
Async XLA Ops:
  6.5 465.4 %all-gather.3.cloned.1.call-start = ((), (), s32[]{:S(2)}) async-start(), calls=%async_computation.1 | async-start | bytes 18874368 | tf_op jit(solution)/shard_map/all_gather | solution.py:40
  31.3 7.6 %copy-start = (s32[16]{0:T(128)S(1)}, s32[16]{0:T(128)}, u32[]{:S(2)}) copy-start(s32[16]{0:T(128)} %param.5) | copy-start | bytes 196
  31.3 425.4 %all-to-all-start = ((bf16[8,3,128,1792]{3,2,1,0:T(8,128)(2,1)}), bf16[8,3,128,1792]{3,2,1,0:T(8,128)(2,1)}, u32[]{:S(2)}, u32[]{:S(2)}) async-start(bf16[8,3,128,1792]{3,2,1,0:T(8,128)(2,1)} %bitcast_dynamic-update-slice_fusion), calls=%async_computation | async-start | bytes 22020096 | tf_op jit(solution)/shard_map/all_to_all | solution.py:13
  38.9 459.7 %all-gather.5.cloned.1.call-start = ((), (), s32[]{:S(2)}) async-start(), calls=%async_computation.2 | async-start | bytes 22020096 | tf_op jit(solution)/shard_map/all_gather | solution.py:21
Sparse Core Ops, SparseCore 0:
  10.9 456.1 all-gather.2
  472.0 26.4 all-gather.4
